TPU v7x, 128 devices: a whole 4x4x4 slice. The times are simulated.
128 devices in a mesh: section: 2 (over x_hi), tensor: 4 (over y), dp: 16 (over z, x_lo, core).
Axes of the slice: x: 4 (x_hi: 2, x_lo: 2; x = x_hi * 2 + x_lo), y: 4, z: 4, core: 2. Of those that a mesh axis runs over, the one named last changes fastest.
Arguments:
- ends: bfloat16 [2, 2, 16, 384, 1024], P('section', None, 'dp', 'tensor'), may hold values from -6 to 6
- lengths: int32 [2, 16, 3], P(None, 'dp'), may hold values from 1 to 336, 384 in all within a row
- qkv_weight: bfloat16 [2, 1024, 3, 1024], P('section', 'dp', None, 'tensor'), may hold values from -0.1875 to 0.1875
- out_weight: bfloat16 [2, 1024, 1024], P('section', 'tensor', 'dp'), may hold values from -2 to 2
- in_weight: bfloat16 [2, 1024, 2, 2624], P('section', 'dp', None, 'tensor'), may hold values from -0.1875 to 0.1875
- down_weight: bfloat16 [2, 2624, 1024], P('section', 'tensor', 'dp'), may hold values from -0.125 to 0.125
- gains: bfloat16 [2, 2, 1024], P('section', None, 'dp'), may hold values from 0.099609375 to 1.8984375
Outputs:
- ends_out: bfloat16 [2, 2, 16, 384, 1024], P('section', None, 'dp', 'tensor')
- grad_qkv: float32 [2, 1024, 3, 1024], P('section', 'dp', None, 'tensor')
- grad_out: float32 [2, 1024, 1024], P('section', 'tensor', 'dp')
- grad_in: float32 [2, 1024, 2, 2624], P('section', 'dp', None, 'tensor')
- grad_down: float32 [2, 2624, 1024], P('section', 'tensor', 'dp')
- grad_gains: float32 [2, 2, 1024], P('section', None, 'dp')
Inputs may be any that keep to these rules, and one draw needn't show every extreme that they name: Each block's 3 lengths sum to 384, and the largest is exactly 336.
All inputs are finite; a program needn't handle non-finite values.
Results may differ from a plain program's by a relative error of at most 0.04.
Values may be sent and summed in bfloat16 or wider, within the bound.
No kernel may reach another device: no remote copies, remote signals or barrier semaphores. Data moves between devices by JAX's collectives and lax.ppermute only.
A program may use at most 128 MiB of HBM per device.

v0:
```python
import jax
import jax.numpy as jnp
from jax import lax
from jax.sharding import PartitionSpec as P

HEAD_DIM = 64
WINDOW = 128


eps_norm = 1e-05


def from_behind(block, axis, distance):
    devices = range(lax.axis_size(axis))
    route = [(i - distance, i) for i in devices if i - distance in devices]
    return lax.ppermute(block, axis, route)


def layer_norm(values, norm_gain):
    centre = values - jnp.mean(values, axis=-1, keepdims=True)
    spread = jnp.mean(centre * centre, axis=-1, keepdims=True)
    return centre * lax.rsqrt(spread + eps_norm) * norm_gain


def doc_layout(lengths, row_count):
    finish = jnp.cumsum(lengths)
    starts = finish - lengths
    row_index = jnp.arange(row_count, dtype=jnp.int32)
    member = (row_index[:, None] >= starts[None, :]) & (row_index[:, None] < finish[None, :])
    doc_ids = jnp.sum(
        jnp.where(member, jnp.arange(lengths.shape[0], dtype=jnp.int32)[None, :], 0), axis=1
    )
    offset = jnp.sum(jnp.where(member, starts[None, :], 0), axis=1)
    return (doc_ids, row_index, row_index - offset)


def rope_tables(positions, rope_base):
    half_dim = HEAD_DIM // 2
    frequency = jnp.exp(
        -(jnp.arange(HEAD_DIM, dtype=jnp.float32) % half_dim)
        * (2.0 * jnp.log(rope_base) / HEAD_DIM)
    )
    angles = positions.astype(jnp.float32)[:, None] * frequency[None, :]
    return (jnp.cos(angles), jnp.sin(angles))


def rotate(heads_in, cos_table, sin_table):
    half_dim = HEAD_DIM // 2
    turned = jnp.concatenate([-heads_in[..., half_dim:], heads_in[..., :half_dim]], axis=-1)
    return heads_in * cos_table[:, None, :] + turned * sin_table[:, None, :]


def rotate_back(grad_heads, cos_table, sin_table):
    half_dim = HEAD_DIM // 2
    scaled = grad_heads * sin_table[:, None, :]
    unturned = jnp.concatenate([scaled[..., half_dim:], -scaled[..., :half_dim]], axis=-1)
    return grad_heads * cos_table[:, None, :] + unturned


def layout_for(doc_lengths, row_count, is_local, rope_base):
    doc_ids, row_index, positions = doc_layout(doc_lengths, row_count)
    near = jnp.abs(row_index[:, None] - row_index[None, :]) <= WINDOW // 2
    allowed = (doc_ids[:, None] == doc_ids[None, :]) & (jnp.logical_not(is_local) | near)
    cos_table, sin_table = rope_tables(positions, rope_base)
    return (allowed, cos_table, sin_table)


def forward_layer(row_block, doc_lengths, weights, is_local, rope_base):
    qkv_w, out_w, in_w, down_w, gain_part = weights
    gain_full = gain_part.astype(jnp.float32)
    normed = layer_norm(row_block, gain_full[0]).astype(jnp.bfloat16)
    normed_all = lax.all_gather(normed, "tensor", axis=0, tiled=True)
    row_count = normed_all.shape[0]
    projected = jnp.einsum("rd,dch->rch", normed_all, qkv_w, preferred_element_type=jnp.float32)
    head_count = projected.shape[2] // HEAD_DIM
    split_heads = projected.reshape(row_count, 3, head_count, HEAD_DIM)
    allowed, cos_table, sin_table = layout_for(doc_lengths, row_count, is_local, rope_base)
    queries = rotate(split_heads[:, 0], cos_table, sin_table).astype(jnp.bfloat16)
    key_rows = rotate(split_heads[:, 1], cos_table, sin_table).astype(jnp.bfloat16)
    value_rows = split_heads[:, 2].astype(jnp.bfloat16)
    score_scale = HEAD_DIM ** (-0.5)
    pieces, log_parts = ([], [])
    scores = (
        jnp.einsum("qhd,khd->hqk", queries, key_rows, preferred_element_type=jnp.float32)
        * score_scale
    )
    masked = jnp.where(allowed[None, 0:row_count], scores, -1e30)
    row_peak = jnp.max(masked, axis=2, keepdims=True)
    exp_scores = jnp.exp(masked - row_peak)
    exp_total = jnp.sum(exp_scores, axis=2, keepdims=True)
    probs = (exp_scores / exp_total).astype(jnp.bfloat16)
    pieces.append(jnp.einsum("hqk,khd->qhd", probs, value_rows, preferred_element_type=jnp.float32))
    log_parts.append(row_peak + jnp.log(exp_total))
    attended = pieces[0].astype(jnp.bfloat16).reshape(row_count, head_count * HEAD_DIM)
    log_total = log_parts[0]
    hidden = row_block + lax.psum_scatter(
        jnp.dot(attended, out_w, preferred_element_type=jnp.float32).astype(jnp.bfloat16),
        "tensor",
        scatter_dimension=0,
        tiled=True,
    ).astype(jnp.float32)
    normed_two = layer_norm(hidden, gain_full[1]).astype(jnp.bfloat16)
    normed_two_all = lax.all_gather(normed_two, "tensor", axis=0, tiled=True)
    lifted = jnp.einsum("rd,dcf->rcf", normed_two_all, in_w, preferred_element_type=jnp.float32)
    activated = (jax.nn.gelu(lifted[:, 0], approximate=False) * lifted[:, 1]).astype(jnp.bfloat16)
    output = hidden + lax.psum_scatter(
        jnp.dot(activated, down_w, preferred_element_type=jnp.float32).astype(jnp.bfloat16),
        "tensor",
        scatter_dimension=0,
        tiled=True,
    ).astype(jnp.float32)
    stored = (
        row_block,
        hidden,
        normed_all,
        queries,
        key_rows,
        value_rows,
        log_total,
        attended,
        normed_two_all,
        lifted,
        activated,
        doc_lengths,
    )
    return (output, stored)


def backward_layer(grad_rows, stored, weights, is_local, rope_base):
    qkv_w, out_w, in_w, down_w, gain_part = weights
    gain_full = gain_part.astype(jnp.float32)
    (
        row_block,
        hidden,
        normed_all,
        queries,
        key_rows,
        value_rows,
        log_total,
        attended,
        normed_two_all,
        lifted,
        activated,
        doc_lengths,
    ) = stored
    row_count = normed_all.shape[0]
    head_count = queries.shape[1]
    grad_all = lax.all_gather(grad_rows.astype(jnp.bfloat16), "tensor", axis=0, tiled=True)
    grad_act = jnp.einsum("rd,fd->rf", grad_all, down_w, preferred_element_type=jnp.float32)
    grad_down = jnp.einsum("rf,rd->fd", activated, grad_all, preferred_element_type=jnp.float32)
    unused, gelu_back = jax.vjp(
        lambda lift_a, lift_b: jax.nn.gelu(lift_a, approximate=False) * lift_b,
        lifted[:, 0],
        lifted[:, 1],
    )
    grad_first, grad_second = gelu_back(grad_act)
    grad_lift = jnp.stack([grad_first, grad_second], axis=1).astype(jnp.bfloat16)
    grad_in = jnp.einsum(
        "rd,rcf->dcf", normed_two_all, grad_lift, preferred_element_type=jnp.float32
    )
    grad_normed_two = lax.psum_scatter(
        jnp.einsum("rcf,dcf->rd", grad_lift, in_w, preferred_element_type=jnp.float32).astype(
            jnp.bfloat16
        ),
        "tensor",
        scatter_dimension=0,
        tiled=True,
    ).astype(jnp.float32)
    unused, norm_back_two = jax.vjp(layer_norm, hidden, gain_full[1])
    grad_hidden_norm, grad_gain_two = norm_back_two(grad_normed_two)
    grad_hidden = grad_rows + grad_hidden_norm
    grad_hidden_all = lax.all_gather(grad_hidden.astype(jnp.bfloat16), "tensor", axis=0, tiled=True)
    grad_out = jnp.einsum(
        "rh,rd->hd", attended, grad_hidden_all, preferred_element_type=jnp.float32
    )
    grad_attended = jnp.einsum(
        "rd,hd->rh", grad_hidden_all, out_w, preferred_element_type=jnp.float32
    )
    grad_attended = grad_attended.astype(jnp.bfloat16).reshape(row_count, head_count, HEAD_DIM)
    allowed, cos_table, sin_table = layout_for(doc_lengths, row_count, is_local, rope_base)
    score_scale = HEAD_DIM ** (-0.5)
    scores = (
        jnp.einsum("qhd,khd->hqk", queries, key_rows, preferred_element_type=jnp.float32)
        * score_scale
    )
    masked = jnp.where(allowed[None, 0:row_count], scores, -1e30)
    probs = jnp.exp(masked - log_total)
    grad_probs = jnp.einsum(
        "qhd,khd->hqk", grad_attended, value_rows, preferred_element_type=jnp.float32
    )
    centred = grad_probs - jnp.sum(grad_probs * probs, axis=2, keepdims=True)
    grad_scores = (probs * centred).astype(jnp.bfloat16)
    grad_query_parts = (
        jnp.einsum("hqk,khd->qhd", grad_scores, key_rows, preferred_element_type=jnp.float32)
        * score_scale
    )
    grad_keys = (
        jnp.einsum("hqk,qhd->khd", grad_scores, queries, preferred_element_type=jnp.float32)
        * score_scale
    )
    grad_values = jnp.einsum(
        "hqk,qhd->khd",
        probs.astype(jnp.bfloat16),
        grad_attended,
        preferred_element_type=jnp.float32,
    )
    grad_proj = jnp.stack(
        [
            rotate_back(grad_query_parts, cos_table, sin_table),
            rotate_back(grad_keys, cos_table, sin_table),
            grad_values,
        ],
        axis=1,
    )
    grad_proj = grad_proj.reshape(row_count, 3, head_count * HEAD_DIM).astype(jnp.bfloat16)
    grad_qkv = jnp.einsum("rd,rch->dch", normed_all, grad_proj, preferred_element_type=jnp.float32)
    grad_normed = lax.psum_scatter(
        jnp.einsum("rch,dch->rd", grad_proj, qkv_w, preferred_element_type=jnp.float32).astype(
            jnp.bfloat16
        ),
        "tensor",
        scatter_dimension=0,
        tiled=True,
    ).astype(jnp.float32)
    unused, norm_back_one = jax.vjp(layer_norm, row_block, gain_full[0])
    grad_rows_norm, grad_gain_one = norm_back_one(grad_normed)
    grad_input = grad_hidden + grad_rows_norm
    return (
        grad_input,
        (grad_qkv, grad_out, grad_in, grad_down, jnp.stack([grad_gain_one, grad_gain_two])),
    )


def body(ends, lengths, qkv_weight, out_weight, in_weight, down_weight, gains):
    section_index = lax.axis_index("section")
    is_local = section_index == 0
    rope_base = jnp.where(is_local, 10000.0, 160000.0).astype(jnp.float32)
    block_rows = ends[0, :, 0]
    layouts = lengths[:, 0]
    micro_count = block_rows.shape[0]
    shard_set = (qkv_weight[0], out_weight[0], in_weight[0], down_weight[0], gains[0])

    def fetch_weights():
        return (
            lax.all_gather(shard_set[0], "dp", axis=0, tiled=True),
            lax.all_gather(shard_set[1], "dp", axis=1, tiled=True),
            lax.all_gather(shard_set[2], "dp", axis=0, tiled=True),
            lax.all_gather(shard_set[3], "dp", axis=1, tiled=True),
            lax.all_gather(shard_set[4], "dp", axis=1, tiled=True),
        )

    zero_rows = jnp.zeros(block_rows.shape[1:], jnp.float32)
    recv_fwd = jnp.zeros(block_rows.shape[1:], jnp.bfloat16)
    recv_back = jnp.zeros(block_rows.shape[1:], jnp.bfloat16)
    stored_steps = {}
    results_low = [None] * micro_count
    results_high = [None] * micro_count
    grad_totals = None
    for step_index in range(micro_count + 2):
        if step_index <= micro_count:
            weights = fetch_weights()
            own_rows = (
                block_rows[step_index].astype(jnp.float32)
                if step_index < micro_count
                else zero_rows
            )
            inputs = jnp.where(is_local, own_rows, recv_fwd.astype(jnp.float32))
            doc_lengths = jnp.where(
                is_local, layouts[min(step_index, micro_count - 1)], layouts[max(step_index - 1, 0)]
            )
            output, stored = forward_layer(inputs, doc_lengths, weights, is_local, rope_base)
            stored_steps[step_index] = stored
            sent_rows = output.astype(jnp.bfloat16)
            if step_index >= 1:
                results_high[step_index - 1] = sent_rows
            if step_index < micro_count:
                recv_fwd = from_behind(sent_rows, "section", 1)
        if step_index >= 1:
            weights = fetch_weights()
            high_index = step_index if step_index <= micro_count else step_index - 2
            low_index = step_index - 2 if step_index >= 2 else step_index
            stored = jax.tree.map(
                lambda first_arg, second_arg: jnp.where(is_local, first_arg, second_arg),
                stored_steps[low_index],
                stored_steps[high_index],
            )
            cotangent = (
                block_rows[step_index - 1].astype(jnp.float32)
                if step_index - 1 < micro_count
                else zero_rows
            )
            came_back = recv_back.astype(jnp.float32) if step_index >= 2 else zero_rows
            grad_rows = jnp.where(is_local, came_back, cotangent)
            grad_input, grads = backward_layer(grad_rows, stored, weights, is_local, rope_base)
            grad_totals = (
                grads if grad_totals is None else jax.tree.map(jnp.add, grad_totals, grads)
            )
            sent_back = grad_input.astype(jnp.bfloat16)
            if step_index >= 2:
                results_low[step_index - 2] = sent_back
            if step_index <= micro_count:
                recv_back = from_behind(sent_back, "section", -1)
    slot_rows = jnp.where(is_local, jnp.stack(results_low), jnp.stack(results_high))
    ends_out = slot_rows[None, :, None]
    gain_total = lax.psum(grad_totals[4], "tensor")
    scattered = (
        lax.psum_scatter(
            grad_totals[0].astype(jnp.bfloat16), "dp", scatter_dimension=0, tiled=True
        ).astype(jnp.float32),
        lax.psum_scatter(
            grad_totals[1].astype(jnp.bfloat16), "dp", scatter_dimension=1, tiled=True
        ).astype(jnp.float32),
        lax.psum_scatter(
            grad_totals[2].astype(jnp.bfloat16), "dp", scatter_dimension=0, tiled=True
        ).astype(jnp.float32),
        lax.psum_scatter(
            grad_totals[3].astype(jnp.bfloat16), "dp", scatter_dimension=1, tiled=True
        ).astype(jnp.float32),
        lax.psum_scatter(
            gain_total.astype(jnp.bfloat16), "dp", scatter_dimension=1, tiled=True
        ).astype(jnp.float32),
    )
    return (
        ends_out,
        scattered[0][None],
        scattered[1][None],
        scattered[2][None],
        scattered[3][None],
        scattered[4][None],
    )


def solution(mesh):
    return jax.shard_map(
        body,
        mesh=mesh,
        in_specs=(
            P("section", None, "dp", "tensor", None),
            P(None, "dp", None),
            P("section", "dp", None, "tensor"),
            P("section", "tensor", "dp"),
            P("section", "dp", None, "tensor"),
            P("section", "tensor", "dp"),
            P("section", None, "dp"),
        ),
        out_specs=(
            P("section", None, "dp", "tensor", None),
            P("section", "dp", None, "tensor"),
            P("section", "tensor", "dp"),
            P("section", "dp", None, "tensor"),
            P("section", "tensor", "dp"),
            P("section", None, "dp"),
        ),
        check_vma=False,
    )
```

profile of v0, /device:TPU:1, one launch (start us, length us, event | category | flops | bytes accessed | tf_op | source)
XLA Modules:
  0.0 1031.9 jit_solution(328238733878034090)
XLA Ops:
  10.8 24.7 %all-gather = bf16[1,2,1024]{1,0,2:T(2,128)(2,1)S(1)} all-gather(bf16[1,2,64]{1,0,2:T(2,128)(2,1)S(1)} %copy.104), channel_id=2, replica_groups=mesh['section'=2,'tensor'=4,'dp'=16] {'dp'}, dimensions={2}, use_global_device_ids=true | all-gather | bytes 4352 | tf_op jit(solution)/shard_map/all_gather | solution.py:249
  46.5 18.6 %all-gather.2 = bf16[1,256,1024]{1,2,0:T(8,128)(2,1)S(1)} all-gather(bf16[1,256,64]{1,2,0:T(8,128)(2,1)S(1)} %copy-done.113), channel_id=4, replica_groups=mesh['section'=2,'tensor'=4,'dp'=16] {'dp'}, dimensions={2}, use_global_device_ids=true | all-gather | bytes 557056 | tf_op jit(solution)/shard_map/all_gather | solution.py:246
  67.3 12.3 %all_gather.35 = bf16[384,1024]{1,0:T(8,128)(2,1)S(1)} all-gather(bf16[96,1024]{1,0:T(8,128)(2,1)S(1)} %fusion.220), channel_id=1, replica_groups=mesh['section'=2,'tensor'=4,'dp'=16] {'tensor'}, dimensions={0}, use_global_device_ids=true | all-gather | bytes 983040 | tf_op jit(solution)/shard_map/all_gather | solution.py:72
  88.8 21.0 %reduce-scatter.20.cloned.1.call-done = bf16[96,1024]{1,0:T(8,128)(2,1)} async-done(((bf16[384,1024]{1,0:T(8,128)(2,1)}), bf16[96,1024]{1,0:T(8,128)(2,1)}) %reduce-scatter.20.cloned.1.call-update) | async-done | bytes 196624 | tf_op jit(solution)/shard_map/reduce_scatter | solution.py:96
  113.1 11.0 %all_gather.38 = bf16[384,1024]{1,0:T(8,128)(2,1)S(1)} all-gather(bf16[96,1024]{1,0:T(8,128)(2,1)S(1)} %multiply_convert_fusion.10), channel_id=1, replica_groups=mesh['section'=2,'tensor'=4,'dp'=16] {'tensor'}, dimensions={0}, use_global_device_ids=true | all-gather | bytes 983040 | tf_op jit(solution)/shard_map/all_gather | solution.py:103
  124.1 24.6 %all-gather.11.cloned.1.call-done = bf16[1,1024,2,656]{3,2,0,1:T(2,128)(2,1)} async-done(((bf16[1,64,2,656]{3,2,0,1:T(2,128)(2,1)}), bf16[1,1024,2,656]{3,2,0,1:T(2,128)(2,1)}) %all-gather.11.cloned.1.call-update) | async-done | bytes 2686992 | tf_op jit(solution)/shard_map/all_gather | solution.py:247
  164.3 19.3 %all-gather.13.cloned.1.call-done = bf16[1,656,1024]{1,2,0:T(8,128)(2,1)} async-done(((bf16[1,656,64]{1,2,0:T(8,128)(2,1)}), bf16[1,656,1024]{1,2,0:T(8,128)(2,1)}) %all-gather.13.cloned.1.call-update) | async-done | bytes 1343504 | tf_op jit(solution)/shard_map/all_gather | solution.py:248
  186.8 21.1 %reduce-scatter.22.cloned.1.call-done = bf16[96,1024]{1,0:T(8,128)(2,1)} async-done(((bf16[384,1024]{1,0:T(8,128)(2,1)}), bf16[96,1024]{1,0:T(8,128)(2,1)}) %reduce-scatter.22.cloned.1.call-update) | async-done | bytes 196624 | tf_op jit(solution)/shard_map/reduce_scatter | solution.py:106
  216.6 12.2 %all_gather.41 = bf16[384,1024]{1,0:T(8,128)(2,1)S(1)} all-gather(bf16[96,1024]{1,0:T(8,128)(2,1)S(1)} %multiply_convert_fusion.9), channel_id=1, replica_groups=mesh['section'=2,'tensor'=4,'dp'=16] {'tensor'}, dimensions={0}, use_global_device_ids=true | all-gather | bytes 983040 | tf_op jit(solution)/shard_map/all_gather | solution.py:72
  236.3 11.4 %all_gather.85 = bf16[384,1024]{1,0:T(8,128)(2,1)} all-gather(bf16[96,1024]{1,0:T(8,128)(2,1)} %get-tuple-element.120), channel_id=1, replica_groups=mesh['section'=2,'tensor'=4,'dp'=16] {'tensor'}, dimensions={0}, use_global_device_ids=true | all-gather | bytes 983040 | tf_op jit(solution)/shard_map/all_gather | solution.py:148
  247.6 13.8 %reduce-scatter.24.cloned.1.call-done = bf16[96,1024]{1,0:T(8,128)(2,1)} async-done(((bf16[384,1024]{1,0:T(8,128)(2,1)}), bf16[96,1024]{1,0:T(8,128)(2,1)}) %reduce-scatter.24.cloned.1.call-update) | async-done | bytes 196624 | tf_op jit(solution)/shard_map/reduce_scatter | solution.py:96
  263.6 12.4 %all_gather.84 = bf16[384,1024]{1,0:T(8,128)(2,1)S(1)} all-gather(bf16[96,1024]{1,0:T(8,128)(2,1)S(1)} %multiply_convert_fusion.8), channel_id=1, replica_groups=mesh['section'=2,'tensor'=4,'dp'=16] {'tensor'}, dimensions={0}, use_global_device_ids=true | all-gather | bytes 983040 | tf_op jit(solution)/shard_map/all_gather | solution.py:103
  288.7 21.2 %reduce-scatter.26.cloned.1.call-done = bf16[96,1024]{1,0:T(8,128)(2,1)} async-done(((bf16[384,1024]{1,0:T(8,128)(2,1)}), bf16[96,1024]{1,0:T(8,128)(2,1)}) %reduce-scatter.26.cloned.1.call-update) | async-done | bytes 196624 | tf_op jit(solution)/shard_map/reduce_scatter | solution.py:161
  309.9 24.6 %reduce-scatter.30.cloned.1.call-done = bf16[96,1024]{1,0:T(8,128)(2,1)} async-done(((bf16[384,1024]{1,0:T(8,128)(2,1)}), bf16[96,1024]{1,0:T(8,128)(2,1)}) %reduce-scatter.30.cloned.1.call-update) | async-done | bytes 196624 | tf_op jit(solution)/shard_map/reduce_scatter | solution.py:106
  339.3 10.8 %all_gather.86 = bf16[384,1024]{1,0:T(8,128)(2,1)S(1)} all-gather(bf16[96,1024]{1,0:T(8,128)(2,1)S(1)} %fusion.265), channel_id=1, replica_groups=mesh['section'=2,'tensor'=4,'dp'=16] {'tensor'}, dimensions={0}, use_global_device_ids=true | all-gather | bytes 983040 | tf_op jit(solution)/shard_map/all_gather | solution.py:172
  377.3 17.0 %reduce-scatter.28.cloned.1.call-done = bf16[96,1024]{1,0:T(8,128)(2,1)} async-done(((bf16[384,1024]{1,0:T(8,128)(2,1)}), bf16[96,1024]{1,0:T(8,128)(2,1)}) %reduce-scatter.28.cloned.1.call-update) | async-done | bytes 196624 | tf_op jit(solution)/shard_map/reduce_scatter | solution.py:217
  395.6 11.2 %all_gather.87 = bf16[384,1024]{1,0:T(8,128)(2,1)S(1)} all-gather(bf16[96,1024]{1,0:T(8,128)(2,1)S(1)} %get-tuple-element.135), channel_id=1, replica_groups=mesh['section'=2,'tensor'=4,'dp'=16] {'tensor'}, dimensions={0}, use_global_device_ids=true | all-gather | bytes 983040 | tf_op jit(solution)/shard_map/all_gather | solution.py:72
  416.8 24.1 %reduce-scatter.32.cloned.1.call-done = bf16[96,1024]{1,0:T(8,128)(2,1)} async-done(((bf16[384,1024]{1,0:T(8,128)(2,1)}), bf16[96,1024]{1,0:T(8,128)(2,1)}) %reduce-scatter.32.cloned.1.call-update) | async-done | bytes 196624 | tf_op jit(solution)/shard_map/reduce_scatter | solution.py:96
  446.6 10.8 %all_gather.88 = bf16[384,1024]{1,0:T(8,128)(2,1)S(1)} all-gather(bf16[96,1024]{1,0:T(8,128)(2,1)S(1)} %multiply_convert_fusion.6), channel_id=1, replica_groups=mesh['section'=2,'tensor'=4,'dp'=16] {'tensor'}, dimensions={0}, use_global_device_ids=true | all-gather | bytes 983040 | tf_op jit(solution)/shard_map/all_gather | solution.py:103
  488.8 23.3 %reduce-scatter.34.cloned.1.call-done = bf16[96,1024]{1,0:T(8,128)(2,1)} async-done(((bf16[384,1024]{1,0:T(8,128)(2,1)}), bf16[96,1024]{1,0:T(8,128)(2,1)}) %reduce-scatter.34.cloned.1.call-update) | async-done | bytes 196624 | tf_op jit(solution)/shard_map/reduce_scatter | solution.py:161
  517.2 11.0 %all_gather.90 = bf16[384,1024]{1,0:T(8,128)(2,1)S(1)} all-gather(bf16[96,1024]{1,0:T(8,128)(2,1)S(1)} %fusion.285), channel_id=1, replica_groups=mesh['section'=2,'tensor'=4,'dp'=16] {'tensor'}, dimensions={0}, use_global_device_ids=true | all-gather | bytes 983040 | tf_op jit(solution)/shard_map/all_gather | solution.py:172
  553.9 19.1 %reduce-scatter.36.cloned.1.call-done = bf16[96,1024]{1,0:T(8,128)(2,1)} async-done(((bf16[384,1024]{1,0:T(8,128)(2,1)}), bf16[96,1024]{1,0:T(8,128)(2,1)}) %reduce-scatter.36.cloned.1.call-update) | async-done | bytes 196624 | tf_op jit(solution)/shard_map/reduce_scatter | solution.py:217
  576.3 21.3 %reduce-scatter.42.cloned.1.call-done = bf16[96,1024]{1,0:T(8,128)(2,1)} async-done(((bf16[384,1024]{1,0:T(8,128)(2,1)}), bf16[96,1024]{1,0:T(8,128)(2,1)}) %reduce-scatter.42.cloned.1.call-update) | async-done | bytes 196624 | tf_op jit(solution)/shard_map/reduce_scatter | solution.py:106
  608.6 12.2 %all_gather.91 = bf16[384,1024]{1,0:T(8,128)(2,1)S(1)} all-gather(bf16[96,1024]{1,0:T(8,128)(2,1)S(1)} %fusion.254), channel_id=1, replica_groups=mesh['section'=2,'tensor'=4,'dp'=16] {'tensor'}, dimensions={0}, use_global_device_ids=true | all-gather | bytes 983040 | tf_op jit(solution)/shard_map/all_gather | solution.py:148
  627.4 23.2 %reduce-scatter.38.cloned.1.call-done = bf16[96,1024]{1,0:T(8,128)(2,1)} async-done(((bf16[384,1024]{1,0:T(8,128)(2,1)}), bf16[96,1024]{1,0:T(8,128)(2,1)}) %reduce-scatter.38.cloned.1.call-update) | async-done | bytes 196624 | tf_op jit(solution)/shard_map/reduce_scatter | solution.py:161
  655.6 11.0 %all_gather.92 = bf16[384,1024]{1,0:T(8,128)(2,1)S(1)} all-gather(bf16[96,1024]{1,0:T(8,128)(2,1)S(1)} %fusion.264), channel_id=1, replica_groups=mesh['section'=2,'tensor'=4,'dp'=16] {'tensor'}, dimensions={0}, use_global_device_ids=true | all-gather | bytes 983040 | tf_op jit(solution)/shard_map/all_gather | solution.py:172
  694.7 11.1 %reduce-scatter.40.cloned.1.call-done = bf16[96,1024]{1,0:T(8,128)(2,1)} async-done(((bf16[384,1024]{1,0:T(8,128)(2,1)}), bf16[96,1024]{1,0:T(8,128)(2,1)}) %reduce-scatter.40.cloned.1.call-update) | async-done | bytes 196624 | tf_op jit(solution)/shard_map/reduce_scatter | solution.py:217
  730.8 35.1 %reduce-scatter.46.cloned.1.call-done = bf16[256,64]{0,1:T(8,128)(2,1)} async-done(((bf16[256,1024]{0,1:T(8,128)(2,1)}), bf16[256,64]{0,1:T(8,128)(2,1)}) %reduce-scatter.46.cloned.1.call-update) | async-done | bytes 32784 | tf_op jit(solution)/shard_map/reduce_scatter | solution.py:310
  767.2 62.8 %reduce-scatter.50.cloned.1.call-done = bf16[656,64]{0,1:T(8,128)(2,1)} async-done(((bf16[656,1024]{0,1:T(8,128)(2,1)}), bf16[656,64]{0,1:T(8,128)(2,1)}) %reduce-scatter.50.cloned.1.call-update) | async-done | bytes 83984 | tf_op jit(solution)/shard_map/reduce_scatter | solution.py:316
  832.7 57.5 %reduce-scatter.52.cloned.1.call-done = bf16[64,2]{1,0:T(8,128)(2,1)} async-done(((bf16[1024,2]{1,0:T(8,128)(2,1)}), bf16[64,2]{1,0:T(8,128)(2,1)}) %reduce-scatter.52.cloned.1.call-update) | async-done | bytes 272
  891.6 63.1 %reduce-scatter.44.cloned.1.call-done = bf16[64,3,256]{2,0,1:T(8,128)(2,1)} async-done(((bf16[1024,3,256]{2,0,1:T(8,128)(2,1)}), bf16[64,3,256]{2,0,1:T(8,128)(2,1)}) %reduce-scatter.44.cloned.1.call-update) | async-done | bytes 98320 | tf_op jit(solution)/shard_map/reduce_scatter | solution.py:307
  956.2 66.4 %reduce-scatter.48.cloned.1.call-done = bf16[64,2,656]{2,0,1:T(8,128)(2,1)} async-done(((bf16[1024,2,656]{2,0,1:T(8,128)(2,1)}), bf16[64,2,656]{2,0,1:T(8,128)(2,1)}) %reduce-scatter.48.cloned.1.call-update) | async-done | bytes 167952 | tf_op jit(solution)/shard_map/reduce_scatter | solution.py:313
  (506 shorter events, 275.7 us)
Async XLA Ops:
  7.2 72.4 %all-gather.9.cloned.1.call-start = ((), (), s32[]{:S(2)}) async-start(), calls=%async_computation.33 | async-start | bytes 1671168 | tf_op jit(solution)/shard_map/all_gather | solution.py:245
  7.9 101.9 %reduce-scatter.20.cloned.1.call-start = ((), (), s32[]{:S(2)}) async-start(), calls=%async_computation.17 | async-start | bytes 983040 | tf_op jit(solution)/shard_map/reduce_scatter | solution.py:96
  87.5 61.3 %all-gather.11.cloned.1.call-start = ((), (), s32[]{:S(2)}) async-start(), calls=%async_computation.34 | async-start | bytes 3342336 | tf_op jit(solution)/shard_map/all_gather | solution.py:247
  88.2 95.3 %all-gather.13.cloned.1.call-start = ((), (), s32[]{:S(2)}) async-start(), calls=%async_computation.35 | async-start | bytes 1671168 | tf_op jit(solution)/shard_map/all_gather | solution.py:248
  88.8 119.1 %reduce-scatter.22.cloned.1.call-start = ((), (), s32[]{:S(2)}) async-start(), calls=%async_computation.18 | async-start | bytes 983040 | tf_op jit(solution)/shard_map/reduce_scatter | solution.py:106
  186.7 74.7 %reduce-scatter.24.cloned.1.call-start = ((), (), s32[]{:S(2)}) async-start(), calls=%async_computation.19 | async-start | bytes 983040 | tf_op jit(solution)/shard_map/reduce_scatter | solution.py:96
  208.9 7.2 collective-permute-start
  216.5 241.0 %copy-start.117 = (f32[96]{0:T(128)}, f32[96]{0:T(128)S(1)}, u32[]{:S(2)}) copy-start(f32[96]{0:T(128)S(1)} %fusion.296) | copy-start | bytes 1156
  236.2 73.7 %reduce-scatter.26.cloned.1.call-start = ((), (), s32[]{:S(2)}) async-start(), calls=%async_computation.20 | async-start | bytes 983040 | tf_op jit(solution)/shard_map/reduce_scatter | solution.py:161
  285.3 49.2 %reduce-scatter.30.cloned.1.call-start = ((), (), s32[]{:S(2)}) async-start(), calls=%async_computation.22 | async-start | bytes 983040 | tf_op jit(solution)/shard_map/reduce_scatter | solution.py:106
  288.7 105.6 %reduce-scatter.28.cloned.1.call-start = ((), (), s32[]{:S(2)}) async-start(), calls=%async_computation.21 | async-start | bytes 983040 | tf_op jit(solution)/shard_map/reduce_scatter | solution.py:217
  368.9 72.1 %reduce-scatter.32.cloned.1.call-start = ((), (), s32[]{:S(2)}) async-start(), calls=%async_computation.23 | async-start | bytes 983040 | tf_op jit(solution)/shard_map/reduce_scatter | solution.py:96
  368.9 7.5 collective-permute-start.2
  415.6 96.5 %reduce-scatter.34.cloned.1.call-start = ((), (), s32[]{:S(2)}) async-start(), calls=%async_computation.24 | async-start | bytes 983040 | tf_op jit(solution)/shard_map/reduce_scatter | solution.py:161
  458.9 8.1 collective-permute-start.1
  484.4 88.6 %reduce-scatter.36.cloned.1.call-start = ((), (), s32[]{:S(2)}) async-start(), calls=%async_computation.25 | async-start | bytes 983040 | tf_op jit(solution)/shard_map/reduce_scatter | solution.py:217
  547.6 50.0 %reduce-scatter.42.cloned.1.call-start = ((), (), s32[]{:S(2)}) async-start(), calls=%async_computation.28 | async-start | bytes 983040 | tf_op jit(solution)/shard_map/reduce_scatter | solution.py:106
  553.8 96.7 %reduce-scatter.38.cloned.1.call-start = ((), (), s32[]{:S(2)}) async-start(), calls=%async_computation.26 | async-start | bytes 983040 | tf_op jit(solution)/shard_map/reduce_scatter | solution.py:161
  600.0 7.9 collective-permute-start.3
  627.3 78.4 %reduce-scatter.40.cloned.1.call-start = ((), (), s32[]{:S(2)}) async-start(), calls=%async_computation.27 | async-start | bytes 983040 | tf_op jit(solution)/shard_map/reduce_scatter | solution.py:217
  680.4 85.5 %reduce-scatter.46.cloned.1.call-start = ((), (), s32[]{:S(2)}) async-start(), calls=%async_computation.30 | async-start | bytes 557056 | tf_op jit(solution)/shard_map/reduce_scatter | solution.py:310
  683.4 146.6 %reduce-scatter.50.cloned.1.call-start = ((), (), s32[]{:S(2)}) async-start(), calls=%async_computation.32 | async-start | bytes 1671168 | tf_op jit(solution)/shard_map/reduce_scatter | solution.py:316
  689.0 201.2 %reduce-scatter.52.cloned.1.call-start = ((), (), s32[]{:S(2)}) async-start(), calls=%async_computation.36 | async-start | bytes 278528
  716.5 238.2 %reduce-scatter.44.cloned.1.call-start = ((), (), s32[]{:S(2)}) async-start(), calls=%async_computation.29 | async-start | bytes 1671168 | tf_op jit(solution)/shard_map/reduce_scatter | solution.py:307
  721.9 300.7 %reduce-scatter.48.cloned.1.call-start = ((), (), s32[]{:S(2)}) async-start(), calls=%async_computation.31 | async-start | bytes 3342336 | tf_op jit(solution)/shard_map/reduce_scatter | solution.py:313
  730.7 101.0 %copy-start.61 = (bf16[96,1024]{1,0:T(8,128)(2,1)S(1)}, bf16[96,1024]{1,0:T(8,128)(2,1)}, u32[]{:S(2)}) copy-start(bf16[96,1024]{1,0:T(8,128)(2,1)} %reduce-scatter.40.cloned.1.call-done) | copy-start | bytes 589828
  730.7 101.0 %copy-start.119 = (f32[96]{0:T(128)S(1)}, f32[96]{0:T(128)}, u32[]{:S(2)}) copy-start(f32[96]{0:T(128)} %copy-done.117) | copy-start | bytes 1156
  730.7 101.0 %copy-start.121 = (f32[96]{0:T(128)S(1)}, f32[96]{0:T(128)}, u32[]{:S(2)}) copy-start(f32[96]{0:T(128)} %copy-done.120) | copy-start | bytes 1156
  730.7 101.0 %copy-start.125 = (f32[96]{0:T(128)S(1)}, f32[96]{0:T(128)}, u32[]{:S(2)}) copy-start(f32[96]{0:T(128)} %copy-done.124) | copy-start | bytes 1156
  730.7 101.2 %copy-start.86 = (bf16[1,1,1,96,1024]{4,3,2,1,0:T(8,128)(2,1)S(1)}, bf16[1,1,1,96,1024]{4,3,2,1,0:T(8,128)(2,1)}, u32[]{:S(2)}) copy-start(bf16[1,1,1,96,1024]{4,3,2,1,0:T(8,128)(2,1)} %get-tuple-element.121) | copy-start | bytes 589828
  730.7 101.2 %copy-start.88 = (bf16[96,1024]{1,0:T(8,128)(2,1)S(1)}, bf16[96,1024]{1,0:T(8,128)(2,1)}, u32[]{:S(2)}) copy-start(bf16[96,1024]{1,0:T(8,128)(2,1)} %copy-done.87) | copy-start | bytes 589828
  730.7 101.2 %copy-start.89 = (bf16[96,1024]{1,0:T(8,128)(2,1)S(1)}, bf16[96,1024]{1,0:T(8,128)(2,1)}, u32[]{:S(2)}) copy-start(bf16[96,1024]{1,0:T(8,128)(2,1)} %get-tuple-element.106) | copy-start | bytes 589828
  (122 other events, 1082.6 us)
Sparse Core Ops, SparseCore 0:
  9.7 37.1 all-gather.8
  87.6 22.1 reduce-scatter.19
  111.5 37.2 all-gather.10
  150.3 33.1 all-gather.12
  186.8 20.9 reduce-scatter.21
  236.3 25.0 reduce-scatter.23
  285.4 24.4 reduce-scatter.25
  312.3 22.1 reduce-scatter.29
  369.0 25.2 reduce-scatter.27
  415.7 25.2 reduce-scatter.31
  484.6 27.5 reduce-scatter.33
  547.7 25.2 reduce-scatter.35
  575.5 22.1 reduce-scatter.41
  627.4 23.1 reduce-scatter.37
  680.5 25.2 reduce-scatter.39
  708.0 57.8 reduce-scatter.45
  768.2 61.7 reduce-scatter.49
  832.2 57.9 reduce-scatter.51
  892.7 61.8 reduce-scatter.43
  956.9 65.7 reduce-scatter.47
where the time goes:
time: 1040 us; the launch traced here: 1030 us
  waiting for transfers between devices  587 us (56%)
  blocking collectives  187 us (18%)
  matrix products  100 us (10%)
  other arithmetic  77.6 us (7%)
  local copies, waits for them, and re-layouts  50.4 us (5%)
  between operations  16.8 us (2%)
  starting transfers between devices  13 us (1%)
    reduce_scatter x3, waiting for transfers between devices, backward_layer(): lax.psum_scatter(jnp.einsum('rcf,dcf->rd', grad_lift, in_w, preferred_ele...  67.7 us
    reduce_scatter x3, waiting for transfers between devices, forward_layer(): lax.psum_scatter(jnp.dot(activated, down_w, preferred_element_type=jnp.fl...  67.1 us
    reduce_scatter x1, waiting for transfers between devices, body(): lax.psum_scatter(grad_totals[2].astype(jnp.bfloat16), 'dp', scatter_dimen...  66.4 us
    reduce_scatter x1, waiting for transfers between devices, body(): lax.psum_scatter(grad_totals[0].astype(jnp.bfloat16), 'dp', scatter_dimen...  63.1 us
    reduce_scatter x1, waiting for transfers between devices, body(): lax.psum_scatter(grad_totals[3].astype(jnp.bfloat16), 'dp', scatter_dimen...  62.8 us
    unnamed x21, waiting for transfers between devices  59.6 us
    reduce_scatter x3, waiting for transfers between devices, forward_layer(): lax.psum_scatter(jnp.dot(attended, out_w, preferred_element_type=jnp.floa...  58.9 us
    reduce_scatter x3, waiting for transfers between devices, backward_layer(): lax.psum_scatter(jnp.einsum('rch,dch->rd', grad_proj, qkv_w, preferred_el...  47.2 us
  transfers between devices with their start and end apart: 24, of which 23 were waited for; matrix products, arithmetic and copies ran while one was open for 9% of the time, Pallas kernels for 0%

commit v1 on v0

v1 whole, which is shorter than its diff:
```python
import jax
import jax.numpy as jnp
from jax import lax
from jax.sharding import PartitionSpec as P

HEAD_DIM = 64
WINDOW = 128
HALF_UNITS = 328
PAD_UNITS = 336
ATTN_ROWS = 544
FF_ROWS = 3 * PAD_UNITS
BF = jnp.bfloat16

eps_norm = 1e-05


def core_swap(value):
    return lax.ppermute(value, "dp", [(i, i ^ 1) for i in range(16)])


def x_swap(value):
    return lax.ppermute(value, "dp", [(i, i ^ 2) for i in range(16)])


def y_shift(value, step):
    return lax.ppermute(value, "tensor", [(i, (i + step) % 4) for i in range(4)])


def z_shift(value, step):
    return lax.ppermute(value, "dp", [(i, (i + 4 * step) % 16) for i in range(16)])


def section_send(value, source, target):
    return lax.ppermute(value, "section", [(source, target)])


def turn(value, shift, axis):
    doubled = jnp.concatenate([value, value], axis=axis)
    return lax.dynamic_slice_in_dim(doubled, shift, value.shape[axis], axis=axis)


def ring_gather(own, shift, cut):
    from_left = shift(own, 1)
    from_right = shift(own, -1)
    far_low = shift(from_left[:cut], 1)
    far_high = shift(from_right[cut:], -1)
    return [own, from_right, (far_low, far_high), from_left]


def ring_reduce(parts, shift, cut):
    own, right, far, left = parts
    far_low = shift(far[:cut], 1)
    far_high = shift(far[cut:], -1)
    right_sum = jnp.concatenate([right[:cut] + far_low, right[cut:]], axis=0)
    left_sum = jnp.concatenate([left[:cut], left[cut:] + far_high], axis=0)
    return own + shift(right_sum, 1) + shift(left_sum, -1)


def gather_chips(own):
    rows = own.shape[0]
    cut = rows // 32 * 16
    other = x_swap(own)
    first_y = ring_gather(own, y_shift, cut)
    first_z = ring_gather(other, z_shift, cut)
    first_y[2] = jnp.concatenate(first_y[2], axis=0)
    first_z[2] = jnp.concatenate(first_z[2], axis=0)
    then_z = ring_gather(jnp.stack(first_y), z_shift, 2)
    then_y = ring_gather(jnp.stack(first_z), y_shift, 2)
    then_z[2] = jnp.concatenate(then_z[2], axis=0)
    then_y[2] = jnp.concatenate(then_y[2], axis=0)
    near = jnp.stack(then_z, axis=2).reshape(4, rows, 4, 1, 128)
    away = jnp.stack([jnp.stack([part[k] for k in range(4)], axis=1) for part in then_y])
    away = away.reshape(4, rows, 4, 1, 128)
    return jnp.concatenate([near, away], axis=3).reshape(4, rows, 1024)


def reduce_chips(full):
    rows = full.shape[1]
    cut = rows // 32 * 16
    blocks = full.reshape(4, rows, 4, 2, 128)
    near = [blocks[:, :, k, 0] for k in range(4)]
    away = [jnp.stack([blocks[t, :, k, 1] for k in range(4)]) for t in range(4)]
    near_z = ring_reduce(near, z_shift, 2)
    away_y = ring_reduce(away, y_shift, 2)
    near_sum = ring_reduce([near_z[k] for k in range(4)], y_shift, cut)
    away_sum = ring_reduce([away_y[k] for k in range(4)], z_shift, cut)
    return near_sum + x_swap(away_sum)


def layer_norm(values, norm_gain):
    centre = values - jnp.mean(values, axis=-1, keepdims=True)
    spread = jnp.mean(centre * centre, axis=-1, keepdims=True)
    return centre * lax.rsqrt(spread + eps_norm) * norm_gain


def doc_layout(lengths, row_index):
    finish = jnp.cumsum(lengths)
    starts = finish - lengths
    member = (row_index[:, None] >= starts[None, :]) & (row_index[:, None] < finish[None, :])
    doc_ids = jnp.sum(
        jnp.where(member, jnp.arange(lengths.shape[0], dtype=jnp.int32)[None, :], 0), axis=1
    )
    offset = jnp.sum(jnp.where(member, starts[None, :], 0), axis=1)
    return (doc_ids, row_index - offset)


def rope_tables(positions, rope_base):
    half_dim = HEAD_DIM // 2
    frequency = jnp.exp(
        -(jnp.arange(HEAD_DIM, dtype=jnp.float32) % half_dim)
        * (2.0 * jnp.log(rope_base) / HEAD_DIM)
    )
    angles = positions.astype(jnp.float32)[:, None] * frequency[None, :]
    return (jnp.cos(angles), jnp.sin(angles))


def rotate(heads_in, cos_table, sin_table):
    half_dim = HEAD_DIM // 2
    turned = jnp.concatenate([-heads_in[..., half_dim:], heads_in[..., :half_dim]], axis=-1)
    return heads_in * cos_table[:, None, :] + turned * sin_table[:, None, :]


def rotate_back(grad_heads, cos_table, sin_table):
    half_dim = HEAD_DIM // 2
    scaled = grad_heads * sin_table[:, None, :]
    unturned = jnp.concatenate([scaled[..., half_dim:], -scaled[..., :half_dim]], axis=-1)
    return grad_heads * cos_table[:, None, :] + unturned


def dot_nt(left, right):
    return lax.dot_general(
        left, right, (((1,), (1,)), ((), ())), preferred_element_type=jnp.float32
    )


def dot_nn(left, right):
    return lax.dot_general(
        left, right, (((1,), (0,)), ((), ())), preferred_element_type=jnp.float32
    )


def dot_tn(left, right):
    return lax.dot_general(
        left, right, (((0,), (0,)), ((), ())), preferred_element_type=jnp.float32
    )


def pair_sum(partial):
    low = partial.astype(BF)
    return low.astype(jnp.float32) + core_swap(low).astype(jnp.float32)


def forward_layer(rows_in, weights, layout):
    qkv_w, out_w, in_a, in_b, down_w, gain_full = weights
    allowed, cos_table, sin_table = layout
    row_count = rows_in.shape[0]
    normed = layer_norm(rows_in, gain_full[0]).astype(BF)
    split_heads = dot_nt(normed, qkv_w).reshape(row_count, 4, 3, 2, HEAD_DIM)
    heads = [split_heads[:, :, k].reshape(row_count, 8, HEAD_DIM) for k in range(3)]
    queries = rotate(heads[0], cos_table, sin_table).astype(BF)
    key_rows = rotate(heads[1], cos_table, sin_table).astype(BF)
    value_rows = heads[2].astype(BF)
    scores = (
        jnp.einsum("qhd,khd->hqk", queries, key_rows, preferred_element_type=jnp.float32)
        * HEAD_DIM ** (-0.5)
    )
    masked = jnp.where(allowed[None], scores, -1e30)
    row_peak = jnp.max(masked, axis=2, keepdims=True)
    exp_scores = jnp.exp(masked - row_peak)
    exp_total = jnp.sum(exp_scores, axis=2, keepdims=True)
    probs = (exp_scores / exp_total).astype(BF)
    attended = jnp.einsum("hqk,khd->qhd", probs, value_rows, preferred_element_type=jnp.float32)
    attended = attended.astype(BF).reshape(row_count, 8 * HEAD_DIM)
    log_total = row_peak + jnp.log(exp_total)
    hidden = rows_in + pair_sum(dot_nn(attended, out_w))
    normed_two = layer_norm(hidden, gain_full[1]).astype(BF)
    lift_a = dot_nt(normed_two, in_a)
    lift_b = dot_nt(normed_two, in_b)
    activated = (jax.nn.gelu(lift_a, approximate=False) * lift_b).astype(BF)
    output = hidden + pair_sum(dot_nn(activated, down_w))
    stored = (
        rows_in,
        hidden,
        normed,
        queries,
        key_rows,
        value_rows,
        log_total,
        attended,
        normed_two,
        lift_a,
        lift_b,
        activated,
    )
    return output, stored


def backward_layer(grad_rows, stored, weights, layout, with_weights):
    qkv_w, out_w, in_a, in_b, down_w, gain_full = weights
    allowed, cos_table, sin_table = layout
    (
        rows_in,
        hidden,
        normed,
        queries,
        key_rows,
        value_rows,
        log_total,
        attended,
        normed_two,
        lift_a,
        lift_b,
        activated,
    ) = stored
    row_count = rows_in.shape[0]
    grads = {}
    grad_low = grad_rows.astype(BF)
    grad_act = dot_nt(grad_low, down_w)
    unused, gelu_back = jax.vjp(
        lambda first, second: jax.nn.gelu(first, approximate=False) * second, lift_a, lift_b
    )
    grad_a, grad_b = gelu_back(grad_act)
    grad_a, grad_b = grad_a.astype(BF), grad_b.astype(BF)
    if with_weights:
        grads["down"] = dot_tn(activated, grad_low).astype(BF)
        grads["in_a"] = dot_tn(grad_a, normed_two).astype(BF)
        grads["in_b"] = dot_tn(grad_b, normed_two).astype(BF)
    grad_normed_two = pair_sum(dot_nn(grad_a, in_a) + dot_nn(grad_b, in_b))
    unused, norm_back_two = jax.vjp(layer_norm, hidden, gain_full[1])
    grad_hidden_norm, grad_gain_two = norm_back_two(grad_normed_two)
    grad_hidden = grad_rows + grad_hidden_norm
    grad_hidden_low = grad_hidden.astype(BF)
    if with_weights:
        grads["out"] = dot_tn(attended, grad_hidden_low).astype(BF)
    grad_attended = dot_nt(grad_hidden_low, out_w).astype(BF)
    grad_attended = grad_attended.reshape(row_count, 8, HEAD_DIM)
    score_scale = HEAD_DIM ** (-0.5)
    scores = (
        jnp.einsum("qhd,khd->hqk", queries, key_rows, preferred_element_type=jnp.float32)
        * score_scale
    )
    masked = jnp.where(allowed[None], scores, -1e30)
    probs = jnp.exp(masked - log_total)
    grad_probs = jnp.einsum(
        "qhd,khd->hqk", grad_attended, value_rows, preferred_element_type=jnp.float32
    )
    centred = grad_probs - jnp.sum(grad_probs * probs, axis=2, keepdims=True)
    grad_scores = (probs * centred).astype(BF)
    grad_queries = (
        jnp.einsum("hqk,khd->qhd", grad_scores, key_rows, preferred_element_type=jnp.float32)
        * score_scale
    )
    grad_keys = (
        jnp.einsum("hqk,qhd->khd", grad_scores, queries, preferred_element_type=jnp.float32)
        * score_scale
    )
    grad_values = jnp.einsum(
        "hqk,qhd->khd", probs.astype(BF), grad_attended, preferred_element_type=jnp.float32
    )
    pieces = [
        rotate_back(grad_queries, cos_table, sin_table),
        rotate_back(grad_keys, cos_table, sin_table),
        grad_values,
    ]
    grad_proj = jnp.stack(
        [piece.reshape(row_count, 4, 2, HEAD_DIM) for piece in pieces], axis=2
    ).astype(BF)
    grad_proj = grad_proj.reshape(row_count, 1536)
    if with_weights:
        grads["qkv"] = dot_tn(grad_proj, normed).astype(BF)
    grad_normed = pair_sum(dot_nn(grad_proj, qkv_w))
    unused, norm_back_one = jax.vjp(layer_norm, rows_in, gain_full[0])
    grad_rows_norm, grad_gain_one = norm_back_one(grad_normed)
    grad_input = grad_hidden + grad_rows_norm
    if with_weights:
        grads["gains"] = jnp.stack([grad_gain_one, grad_gain_two]).astype(BF)
    return grad_input, grads


def body(ends, lengths, qkv_weight, out_weight, in_weight, down_weight, gains):
    is_local = lax.axis_index("section") == 0
    row_part = lax.axis_index("tensor")
    dp_index = lax.axis_index("dp")
    on_first = dp_index % 2 == 0
    x_first = (dp_index // 2) % 2 == 0
    z_part = dp_index // 4
    rope_base = jnp.where(is_local, 10000.0, 160000.0).astype(jnp.float32)

    def by_core(low, high):
        return jnp.where(on_first, low, high)

    def paired(own, came, axis):
        return jnp.concatenate([by_core(own, came), by_core(came, own)], axis=axis)

    def halves(low, high):
        return by_core(low, high), core_swap(by_core(high, low))

    def pad_units(value):
        return jnp.pad(value, ((0, 0), (0, PAD_UNITS - HALF_UNITS), (0, 0)))

    qkv_t = qkv_weight[0].transpose(1, 2, 0).reshape(3, 2, 128, 64)
    out_t = out_weight[0].reshape(1, 2, 128, 64)
    attn_t = jnp.concatenate([qkv_t, out_t], axis=0).reshape(4, 2, 128, 64)
    gain_rows = jnp.pad(gains[0], ((0, 30), (0, 0)))
    attn_low = jnp.concatenate([attn_t[:, 0].reshape(512, 64), gain_rows], axis=0)
    attn_high = jnp.concatenate([attn_t[:, 1].reshape(512, 64), gain_rows], axis=0)
    attn_own = paired(*halves(attn_low, attn_high), axis=1)
    in_t = in_weight[0].transpose(1, 2, 0).reshape(2, 2, HALF_UNITS, 64)
    down_t = down_weight[0].reshape(1, 2, HALF_UNITS, 64)
    ff_t = jnp.concatenate([in_t, down_t], axis=0)
    ff_low = pad_units(ff_t[:, 0]).reshape(FF_ROWS, 64)
    ff_high = pad_units(ff_t[:, 1]).reshape(FF_ROWS, 64)
    ff_own = paired(*halves(ff_low, ff_high), axis=1)

    def to_own(value):
        split = value.reshape(*value.shape[:-1], 4, 2, 128)
        split = jnp.where(x_first, split, split[..., ::-1, :])
        return turn(split, z_part, split.ndim - 3).reshape(value.shape)

    def from_own(value):
        split = value.reshape(*value.shape[:-1], 4, 2, 128)
        split = turn(split, (4 - z_part) % 4, split.ndim - 3)
        return jnp.where(x_first, split, split[..., ::-1, :]).reshape(value.shape)

    rows_here = to_own(ends[0, :, 0])
    kept, came = halves(rows_here[..., :512], rows_here[..., 512:])
    by_block = jnp.stack([by_core(kept, came), by_core(came, kept)], axis=1)
    by_block = turn(by_block.reshape(4, 96, 512), row_part, 0)
    half_rows = [by_block[0]] + [y_shift(by_block[(4 - k) % 4], -k) for k in (1, 2, 3)]
    half_rows = jnp.concatenate(half_rows, axis=0)
    block_rows = paired(half_rows, core_swap(half_rows), axis=1).astype(jnp.float32)

    own_lengths = lengths[:, 0]
    both_lengths = jnp.stack([own_lengths, core_swap(own_lengths)], axis=1)
    wanted = row_part % 2 == dp_index % 2
    both_lengths = jnp.where(wanted, both_lengths[:, 0], both_lengths[:, 1])
    doc_lengths = jnp.where(row_part // 2 == 0, both_lengths[0], both_lengths[1])
    local_rows = jnp.arange(384, dtype=jnp.int32)
    row_index = 96 * ((row_part + local_rows // 96) % 4) + local_rows % 96
    doc_ids, positions = doc_layout(doc_lengths, row_index)
    near = jnp.abs(row_index[:, None] - row_index[None, :]) <= WINDOW // 2
    allowed = (doc_ids[:, None] == doc_ids[None, :]) & (jnp.logical_not(is_local) | near)
    layout = (allowed, *rope_tables(positions, rope_base))

    attn_full = gather_chips(attn_own)
    ff_full = gather_chips(ff_own)
    weights = (
        attn_full[:, :384].reshape(1536, 1024),
        attn_full[:, 384:512].reshape(512, 1024),
        ff_full[:, :PAD_UNITS].reshape(4 * PAD_UNITS, 1024),
        ff_full[:, PAD_UNITS : 2 * PAD_UNITS].reshape(4 * PAD_UNITS, 1024),
        ff_full[:, 2 * PAD_UNITS :].reshape(4 * PAD_UNITS, 1024),
        attn_full[0, 512:514].astype(jnp.float32),
    )

    def relay(rows, source, target):
        sent = section_send(by_core(rows[:192], rows[192:]), source, target)
        return paired(sent, core_swap(sent), axis=0).astype(jnp.float32)

    first_out, unused = forward_layer(block_rows, weights, layout)
    second_in = jnp.where(is_local, block_rows, relay(first_out.astype(BF), 0, 1))
    output, stored = forward_layer(second_in, weights, layout)
    grad_last, unused = backward_layer(block_rows, stored, weights, layout, False)
    grad_rows = jnp.where(is_local, relay(grad_last.astype(BF), 1, 0), block_rows)
    grad_input, grads = backward_layer(grad_rows, stored, weights, layout, True)

    ff_grads = jnp.concatenate(
        [grads[name].reshape(4, PAD_UNITS, 1024) for name in ("in_a", "in_b", "down")], axis=1
    )
    ff_sum = reduce_chips(ff_grads)
    gain_grads = jnp.pad(grads["gains"], ((0, 30), (0, 0)))
    attn_grads = jnp.concatenate(
        [
            grads["qkv"].reshape(4, 384, 1024),
            grads["out"].reshape(4, 128, 1024),
            jnp.broadcast_to(gain_grads[None], (4, 32, 1024)),
        ],
        axis=1,
    )
    attn_sum = reduce_chips(attn_grads)

    def own_units(value, count):
        kept, came = halves(value[:, :64], value[:, 64:])
        low, high = by_core(kept, came), by_core(came, kept)
        return low.reshape(count, -1, 64), high.reshape(count, -1, 64)

    ff_low, ff_high = own_units(ff_sum, 3)
    ff_both = jnp.concatenate([ff_low[:, :HALF_UNITS], ff_high[:, :HALF_UNITS]], axis=1)
    ff_both = ff_both.astype(jnp.float32)
    attn_low, attn_high = own_units(attn_sum[:512], 4)
    attn_both = jnp.concatenate([attn_low, attn_high], axis=1).astype(jnp.float32)
    gain_out = by_core(attn_sum[512:514, :64], attn_sum[512:514, 64:]).astype(jnp.float32)

    result = jnp.where(is_local, grad_input, output).astype(BF)
    half_out = by_core(result[:, :512], result[:, 512:]).reshape(4, 96, 512)
    back = [half_out[0]] + [y_shift(half_out[k], k) for k in (1, 2, 3)]
    back = jnp.stack([back[0], back[3], back[2], back[1]])
    back = turn(back, (4 - row_part) % 4, 0).reshape(2, 2, 96, 512)
    kept, came = halves(back[:, 0], back[:, 1])
    ends_out = from_own(paired(kept, came, axis=2))

    return (
        ends_out[None, :, None],
        attn_both[:3].transpose(2, 0, 1)[None],
        attn_both[3][None],
        ff_both[:2].transpose(2, 0, 1)[None],
        ff_both[2][None],
        gain_out[None],
    )


def solution(mesh):
    return jax.shard_map(
        body,
        mesh=mesh,
        in_specs=(
            P("section", None, "dp", "tensor", None),
            P(None, "dp", None),
            P("section", "dp", None, "tensor"),
            P("section", "tensor", "dp"),
            P("section", "dp", None, "tensor"),
            P("section", "tensor", "dp"),
            P("section", None, "dp"),
        ),
        out_specs=(
            P("section", None, "dp", "tensor", None),
            P("section", "dp", None, "tensor"),
            P("section", "tensor", "dp"),
            P("section", "dp", None, "tensor"),
            P("section", "tensor", "dp"),
            P("section", None, "dp"),
        ),
        check_vma=False,
    )
```

time: 1040 us -> 682 us (0.66)
  waiting for transfers between devices: 587 us -> 71.1 us
  local copies, waits for them, and re-layouts: 50.4 us -> 251 us
  blocking collectives: 187 us -> 0 us
  starting transfers between devices: 13 us -> 130 us
  other arithmetic: 77.6 us -> 112 us
  between operations: 16.8 us -> 3.8 us
    reduce_scatter x16 -> x0, waiting for transfers between devices: 468 us -> none  [the longest x3 67.7 us: backward_layer(): lax.psum_scatter(jnp.einsum('rcf,dcf->rd', grad_lift, in_w, preferred_ele...]
    all_gather x14 -> x0, blocking collectives: 181 us -> none  [the longest x3 35.8 us: forward_layer(): normed_all = lax.all_gather(normed, 'tensor', axis=0, tiled=True)]
    ppermute x4 -> x94, starting transfers between devices: 11.9 us -> 130 us  [the longest x38 47.9 us: y_shift(): lax.ppermute(value, 'tensor', [(i, (i + step) % 4) for i in range(4)])]
    concatenate x0 -> x18, local copies, waits for them, and re-layouts: none -> 93.8 us  [the longest x6 48.6 us: body(): jnp.concatenate([grads[name].reshape(4, PAD_UNITS, 1024) for name in ('in...]
    unnamed x21 -> x0, waiting for transfers between devices: 59.6 us -> none
    ppermute x4 -> x94, waiting for transfers between devices: 14.8 us -> 71.1 us  [the longest x38 31.1 us: y_shift(): lax.ppermute(value, 'tensor', [(i, (i + step) % 4) for i in range(4)])]
    slice x1 -> x41, local copies, waits for them, and re-layouts: 6.15 us -> 52.4 us  [the longest x2 12.9 us: body(): ff_full[:, :PAD_UNITS].reshape(4 * PAD_UNITS, 1024)]
    all_gather x3 -> x0, waiting for transfers between devices: 43.9 us -> none  [the longest x1 24.6 us: fetch_weights(): lax.all_gather(shard_set[2], 'dp', axis=0, tiled=True)]
  transfers between devices with their start and end apart: 24 -> 94, of which waited for: 23 -> 23; matrix products, arithmetic and copies ran while one was open for 9% -> 52% of each run, Pallas kernels for 0% -> 0%
where the time goes in v1:
time: 682 us; the launch traced here: 669 us
  local copies, waits for them, and re-layouts  251 us (37%)
  starting transfers between devices  130 us (19%)
  other arithmetic  112 us (16%)
  matrix products  101 us (15%)
  waiting for transfers between devices  71.1 us (10%)
    unnamed x275, local copies, waits for them, and re-layouts  52.3 us
    concatenate x6, local copies, waits for them, and re-layouts, body(): jnp.concatenate([grads[name].reshape(4, PAD_UNITS, 1024) for name in ('in...  48.6 us
    ppermute x38, starting transfers between devices, y_shift(): lax.ppermute(value, 'tensor', [(i, (i + step) % 4) for i in range(4)])  47.9 us
    ppermute x32, starting transfers between devices, z_shift(): lax.ppermute(value, 'dp', [(i, (i + 4 * step) % 16) for i in range(16)])  37.5 us
    ppermute x18, starting transfers between devices, core_swap(): return lax.ppermute(value, 'dp', [(i, i ^ 1) for i in range(16)])  34.6 us
    ppermute x38, waiting for transfers between devices, y_shift(): lax.ppermute(value, 'tensor', [(i, (i + step) % 4) for i in range(4)])  31.1 us
    dot_general x10, matrix products, dot_nn(): lax.dot_general(left, right, (((1,), (0,)), ((), ())), preferred_element_...  28.8 us
    dot_general x9, matrix products, dot_nt(): lax.dot_general(left, right, (((1,), (1,)), ((), ())), preferred_element_...  25.9 us
  transfers between devices with their start and end apart: 94, of which 23 were waited for; matrix products, arithmetic and copies ran while one was open for 52% of the time, Pallas kernels for 0%

profile of v1, /device:TPU:1, one launch (start us, length us, event | category | flops | bytes accessed | tf_op | source)
XLA Modules:
  0.0 669.3 jit_solution(4574548776379617644)
XLA Ops:
  68.6 5.7 collective-permute-done.37
  129.3 11.9 %copy.390 = bf16[4,544,4,2,128]{4,3,2,1,0:T(2,128)(2,1)} copy(bf16[4,544,4,2,128]{1,4,0,2,3:T(8,128)(2,1)} %pad_maximum_fusion.2) | data formatting | bytes 8912896 | tf_op jit(solution)/shard_map/concatenate | solution.py:74
  141.2 10.7 %reshape.526 = bf16[4,544,1024]{2,1,0:T(8,128)(2,1)} reshape(bf16[4,544,4,2,128]{4,3,2,1,0:T(2,128)(2,1)} %copy.390) | data formatting | bytes 8912896 | tf_op jit(solution)/shard_map/reshape | solution.py:74
  159.1 5.0 fusion.266
  169.3 4.6 collective-permute-start.24
  220.7 5.1 collective-permute-done.42
  228.3 6.3 pad_maximum_fusion
  234.6 8.3 %copy.413 = bf16[4,1008,4,2,128]{1,4,3,2,0:T(8,128)(2,1)} copy(bf16[4,1008,4,2,128]{1,4,2,0,3:T(8,128)(2,1)} %pad_maximum_fusion) | data formatting | bytes 16515072 | tf_op jit(solution)/shard_map/concatenate | solution.py:74
  242.8 8.3 %fusion.252 = (bf16[4,336,1024]{1,2,0:T(8,128)(2,1)}, bf16[4,336,1024]{1,2,0:T(8,128)(2,1)}, bf16[4,336,1024]{1,2,0:T(8,128)(2,1)}) fusion(bf16[4,1008,1024]{1,2,0:T(8,128)(2,1)} %bitcast.584), kind=kLoop, calls=%fused_computation.605 | loop fusion | bytes 16515072 | tf_op jit(solution)/shard_map/slice | solution.py:350
  251.1 4.6 copy.414
  255.7 4.6 copy.416
  263.6 6.0 fusion.267
  269.6 10.6 %fusion.64 = bf16[384,1024]{1,0:T(8,128)(2,1)} fusion(bf16[1344,1024]{1,0:T(8,128)(2,1)} %bitcast.615, bf16[384,1024]{1,0:T(8,128)(2,1)} %multiply_convert_fusion.7, bf16[1344,1024]{1,0:T(8,128)(2,1)S(1)} %bitcast.585, f32[384,1344]{0,1:T(8,128)} %fusion.267), kind=kOutput, calls=%fused_computation.149 | convolution fusion | flops 2148384768 | bytes 9142272 | tf_op jit(solution)/shard_map/dot_general | solution.py:137
  286.4 4.9 collective-permute-start.44
  291.3 8.1 %collective-permute-done.44 = bf16[192,1024]{1,0:T(8,128)(2,1)S(1)} collective-permute-done((bf16[192,1024]{1,0:T(8,128)(2,1)S(1)}, bf16[192,1024]{1,0:T(8,128)(2,1)S(1)}, u32[]{:S(2)}, u32[]{:S(2)}) %collective-permute-start.44) | collective-permute-done | bytes 393248 | tf_op jit(solution)/shard_map/ppermute | solution.py:34
  320.0 6.6 multiply_convert_fusion.2
  361.4 13.0 %collective-permute-done.49 = bf16[192,1024]{1,0:T(8,128)(2,1)} collective-permute-done((bf16[192,1024]{1,0:T(8,128)(2,1)}, bf16[192,1024]{1,0:T(8,128)(2,1)}, u32[]{:S(2)}, u32[]{:S(2)}) %collective-permute-start.49) | collective-permute-done | bytes 393248 | tf_op jit(solution)/shard_map/ppermute | solution.py:34
  375.6 4.6 convolution_convert_fusion.5
  393.7 7.6 %concatenate.227 = bf16[4,336,4,2,128]{4,3,2,1,0:T(2,128)(2,1)} reshape(bf16[1344,1024]{1,0:T(8,128)(2,1)} %convolution_convert_fusion) | data formatting | bytes 5505024 | tf_op jit(solution)/shard_map/concatenate | solution.py:367
  401.3 8.7 %copy.449 = bf16[4,336,4,2,128]{1,4,3,2,0:T(8,128)(2,1)} copy(bf16[4,336,4,2,128]{4,3,2,1,0:T(2,128)(2,1)} %concatenate.227) | data formatting | bytes 5505024 | tf_op jit(solution)/shard_map/concatenate | solution.py:367
  410.0 4.6 convolution_convert_fusion.1
  414.5 7.4 %concatenate.226 = bf16[4,336,4,2,128]{4,3,2,1,0:T(2,128)(2,1)} reshape(bf16[1344,1024]{1,0:T(8,128)(2,1)} %convolution_convert_fusion.1) | data formatting | bytes 5505024 | tf_op jit(solution)/shard_map/concatenate | solution.py:367
  421.9 8.7 %copy.448 = bf16[4,336,4,2,128]{1,4,3,2,0:T(8,128)(2,1)} copy(bf16[4,336,4,2,128]{4,3,2,1,0:T(2,128)(2,1)} %concatenate.226) | data formatting | bytes 5505024 | tf_op jit(solution)/shard_map/concatenate | solution.py:367
  430.6 7.4 %concatenate.225 = bf16[4,336,4,2,128]{4,3,2,1,0:T(2,128)(2,1)} reshape(bf16[1344,1024]{1,0:T(8,128)(2,1)} %convolution_convert_fusion.2) | data formatting | bytes 5505024 | tf_op jit(solution)/shard_map/concatenate | solution.py:367
  438.0 8.8 %copy.447 = bf16[4,336,4,2,128]{1,4,3,2,0:T(8,128)(2,1)} copy(bf16[4,336,4,2,128]{4,3,2,1,0:T(2,128)(2,1)} %concatenate.225) | data formatting | bytes 5505024 | tf_op jit(solution)/shard_map/concatenate | solution.py:367
  452.9 5.1 pad_maximum_fusion.1
  467.6 8.7 %collective-permute-done.84 = bf16[2,1008,128]{1,2,0:T(8,128)(2,1)S(1)} collective-permute-done((bf16[2,1008,128]{1,2,0:T(8,128)(2,1)S(1)}, bf16[2,1008,128]{1,2,0:T(8,128)(2,1)S(1)}, u32[]{:S(2)}, u32[]{:S(2)}) %collective-permute-start.84) | collective-permute-done | bytes 516128 | tf_op jit(solution)/shard_map/ppermute | solution.py:26
  511.9 4.7 fusion.69
  535.4 6.1 concatenate.213
  541.5 4.5 copy.437
  605.6 5.5 collective-permute-start.57
  660.0 6.0 collective-permute-start.75
  (753 shorter events, 443.1 us)
Async XLA Ops:
  43.2 20.3 %collective-permute-start.4 = (bf16[384,512]{1,0:T(8,128)(2,1)}, bf16[384,512]{1,0:T(8,128)(2,1)}, u32[]{:S(2)}, u32[]{:S(2)}) collective-permute-start(bf16[384,512]{1,0:T(8,128)(2,1)} %pad_maximum_fusion.23), channel_id=1, source_target_pairs={{0,1},{1,0},{2,3},{3,2},{4,5},{5,4},{6,7},{7,6},{8,9},{9,8},{10,11... | collective-permute-start | bytes 1179656 | tf_op jit(solution)/shard_map/ppermute | solution.py:18
  54.9 26.0 %collective-permute-start.11 = (bf16[4,544,128]{2,1,0:T(8,128)(2,1)}, bf16[4,544,128]{2,1,0:T(8,128)(2,1)}, u32[]{:S(2)}, u32[]{:S(2)}) collective-permute-start(bf16[4,544,128]{2,1,0:T(8,128)(2,1)} %copy.370), channel_id=1, source_target_pairs={{0,4},{1,5},{2,6},{3,7},{4,8},{5,9},{6,10},{7,11},{8,12},{9,13},{1... | collective-permute-start | bytes 1671176 | tf_op jit(solution)/shard_map/ppermute | solution.py:30
  54.9 30.8 %collective-permute-start.10 = (bf16[4,544,128]{2,1,0:T(8,128)(2,1)}, bf16[4,544,128]{2,1,0:T(8,128)(2,1)}, u32[]{:S(2)}, u32[]{:S(2)}) collective-permute-start(bf16[4,544,128]{2,1,0:T(8,128)(2,1)} %copy.370), channel_id=1, source_target_pairs={{0,12},{1,13},{2,14},{3,15},{4,0},{5,1},{6,2},{7,3},{8,4},{9,5},{1... | collective-permute-start | bytes 1671176 | tf_op jit(solution)/shard_map/ppermute | solution.py:30
  62.3 25.9 %collective-permute-start.20 = (bf16[4,544,128]{2,1,0:T(8,128)(2,1)}, bf16[4,544,128]{2,1,0:T(8,128)(2,1)}, u32[]{:S(2)}, u32[]{:S(2)}) collective-permute-start(bf16[4,544,128]{2,1,0:T(8,128)(2,1)} %copy.376), channel_id=1, source_target_pairs={{0,16},{16,32},{32,48},{48,0},{1,17},{17,33},{33,49},{49,1},{2,18}... | collective-permute-start | bytes 1671176 | tf_op jit(solution)/shard_map/ppermute | solution.py:26
  75.4 98.6 %collective-permute-start.31 = (bf16[4,1008,128]{2,1,0:T(8,128)(2,1)}, bf16[4,1008,128]{2,1,0:T(8,128)(2,1)}, u32[]{:S(2)}, u32[]{:S(2)}) collective-permute-start(bf16[4,1008,128]{2,1,0:T(8,128)(2,1)} %copy.395), channel_id=1, source_target_pairs={{0,4},{1,5},{2,6},{3,7},{4,8},{5,9},{6,10},{7,11},{8,12},{9,13},{1... | collective-permute-start | bytes 3096584 | tf_op jit(solution)/shard_map/ppermute | solution.py:30
  80.9 95.4 %collective-permute-start.30 = (bf16[4,1008,128]{2,1,0:T(8,128)(2,1)}, bf16[4,1008,128]{2,1,0:T(8,128)(2,1)}, u32[]{:S(2)}, u32[]{:S(2)}) collective-permute-start(bf16[4,1008,128]{2,1,0:T(8,128)(2,1)} %copy.395), channel_id=1, source_target_pairs={{0,12},{1,13},{2,14},{3,15},{4,0},{5,1},{6,2},{7,3},{8,4},{9,5},{1... | collective-permute-start | bytes 3096584 | tf_op jit(solution)/shard_map/ppermute | solution.py:30
  85.7 97.4 %collective-permute-start.40 = (bf16[4,1008,128]{2,1,0:T(8,128)(2,1)}, bf16[4,1008,128]{2,1,0:T(8,128)(2,1)}, u32[]{:S(2)}, u32[]{:S(2)}) collective-permute-start(bf16[4,1008,128]{2,1,0:T(8,128)(2,1)} %copy.401), channel_id=1, source_target_pairs={{0,16},{16,32},{32,48},{48,0},{1,17},{17,33},{33,49},{49,1},{2,18}... | collective-permute-start | bytes 3096584 | tf_op jit(solution)/shard_map/ppermute | solution.py:26
  88.2 29.9 %collective-permute-start.12 = (bf16[2,544,128]{1,2,0:T(8,128)(2,1)}, bf16[2,544,128]{1,2,0:T(8,128)(2,1)}, u32[]{:S(2)}, u32[]{:S(2)}) collective-permute-start(bf16[2,544,128]{1,2,0:T(8,128)(2,1)} %slice.972), channel_id=1, source_target_pairs={{0,4},{1,5},{2,6},{3,7},{4,8},{5,9},{6,10},{7,11},{8,12},{9,13},{1... | collective-permute-start | bytes 835592 | tf_op jit(solution)/shard_map/ppermute | solution.py:30
  90.2 28.1 %collective-permute-start.13 = (bf16[2,544,128]{1,2,0:T(8,128)(2,1)}, bf16[2,544,128]{1,2,0:T(8,128)(2,1)}, u32[]{:S(2)}, u32[]{:S(2)}) collective-permute-start(bf16[2,544,128]{1,2,0:T(8,128)(2,1)} %slice.973), channel_id=1, source_target_pairs={{0,12},{1,13},{2,14},{3,15},{4,0},{5,1},{6,2},{7,3},{8,4},{9,5},{1... | collective-permute-start | bytes 835592 | tf_op jit(solution)/shard_map/ppermute | solution.py:30
  125.4 73.0 %collective-permute-start.39 = (bf16[4,1008,128]{2,1,0:T(8,128)(2,1)}, bf16[4,1008,128]{2,1,0:T(8,128)(2,1)}, u32[]{:S(2)}, u32[]{:S(2)}) collective-permute-start(bf16[4,1008,128]{2,1,0:T(8,128)(2,1)} %copy.401), channel_id=1, source_target_pairs={{0,48},{16,0},{32,16},{48,32},{1,49},{17,1},{33,17},{49,33},{2,50}... | collective-permute-start | bytes 3096584 | tf_op jit(solution)/shard_map/ppermute | solution.py:26
  169.3 46.0 %collective-permute-start.24 = (bf16[384,1024]{1,0:T(8,128)(2,1)S(1)}, bf16[384,1024]{1,0:T(8,128)(2,1)S(1)}, u32[]{:S(2)}, u32[]{:S(2)}) collective-permute-start(bf16[384,1024]{1,0:T(8,128)(2,1)S(1)} %convolution_convert_fusion.9), channel_id=1, source_target_pairs={{0,1},{1,0},{2,3},{3,2},{4,5},{5,4},{6,7},{7,6},{8,9},{9,8},{10,11... | collective-permute-start | bytes 2359304 | tf_op jit(solution)/shard_map/ppermute | solution.py:18
  176.3 41.3 %collective-permute-start.32 = (bf16[2,1008,128]{1,2,0:T(8,128)(2,1)}, bf16[2,1008,128]{1,2,0:T(8,128)(2,1)}, u32[]{:S(2)}, u32[]{:S(2)}) collective-permute-start(bf16[2,1008,128]{1,2,0:T(8,128)(2,1)} %slice.1006), channel_id=1, source_target_pairs={{0,4},{1,5},{2,6},{3,7},{4,8},{5,9},{6,10},{7,11},{8,12},{9,13},{1... | collective-permute-start | bytes 1548296 | tf_op jit(solution)/shard_map/ppermute | solution.py:30
  180.5 37.2 %collective-permute-start.33 = (bf16[2,1008,128]{1,2,0:T(8,128)(2,1)}, bf16[2,1008,128]{1,2,0:T(8,128)(2,1)}, u32[]{:S(2)}, u32[]{:S(2)}) collective-permute-start(bf16[2,1008,128]{1,2,0:T(8,128)(2,1)} %slice.1007), channel_id=1, source_target_pairs={{0,12},{1,13},{2,14},{3,15},{4,0},{5,1},{6,2},{7,3},{8,4},{9,5},{1... | collective-permute-start | bytes 1548296 | tf_op jit(solution)/shard_map/ppermute | solution.py:30
  196.5 23.0 %collective-permute-start.41 = (bf16[2,1008,128]{1,2,0:T(8,128)(2,1)}, bf16[2,1008,128]{1,2,0:T(8,128)(2,1)}, u32[]{:S(2)}, u32[]{:S(2)}) collective-permute-start(bf16[2,1008,128]{1,2,0:T(8,128)(2,1)} %copy.501), channel_id=1, source_target_pairs={{0,16},{16,32},{32,48},{48,0},{1,17},{17,33},{33,49},{49,1},{2,18}... | collective-permute-start | bytes 1548296 | tf_op jit(solution)/shard_map/ppermute | solution.py:26
  380.2 195.0 %collective-permute-start.53 = (bf16[384,1024]{1,0:T(8,128)(2,1)}, bf16[384,1024]{1,0:T(8,128)(2,1)}, u32[]{:S(2)}, u32[]{:S(2)}) collective-permute-start(bf16[384,1024]{1,0:T(8,128)(2,1)} %convolution_convert_fusion.5), channel_id=1, source_target_pairs={{0,1},{1,0},{2,3},{3,2},{4,5},{5,4},{6,7},{7,6},{8,9},{9,8},{10,11... | collective-permute-start | bytes 2359304 | tf_op jit(solution)/shard_map/ppermute | solution.py:18
  460.9 40.4 %collective-permute-start.51 = (bf16[384,1024]{1,0:T(8,128)(2,1)}, bf16[384,1024]{1,0:T(8,128)(2,1)}, u32[]{:S(2)}, u32[]{:S(2)}) collective-permute-start(bf16[384,1024]{1,0:T(8,128)(2,1)} %add_convert_fusion.2), channel_id=1, source_target_pairs={{0,1},{1,0},{2,3},{3,2},{4,5},{5,4},{6,7},{7,6},{8,9},{9,8},{10,11... | collective-permute-start | bytes 2359304 | tf_op jit(solution)/shard_map/ppermute | solution.py:18
  466.4 19.7 %collective-permute-start.76 = (bf16[2,1008,128]{1,2,0:T(8,128)(2,1)}, bf16[2,1008,128]{1,2,0:T(8,128)(2,1)}, u32[]{:S(2)}, u32[]{:S(2)}) collective-permute-start(bf16[2,1008,128]{1,2,0:T(8,128)(2,1)} %get-tuple-element.68), channel_id=1, source_target_pairs={{0,4},{1,5},{2,6},{3,7},{4,8},{5,9},{6,10},{7,11},{8,12},{9,13},{1... | collective-permute-start | bytes 1548296 | tf_op jit(solution)/shard_map/ppermute | solution.py:30
  480.2 68.1 %collective-permute-start.85 = (bf16[4,1008,128]{2,1,0:T(8,128)(2,1)}, bf16[4,1008,128]{2,1,0:T(8,128)(2,1)}, u32[]{:S(2)}, u32[]{:S(2)}) collective-permute-start(bf16[4,1008,128]{2,1,0:T(8,128)(2,1)} %copy.458), channel_id=1, source_target_pairs={{0,16},{16,32},{32,48},{48,0},{1,17},{17,33},{33,49},{49,1},{2,18}... | collective-permute-start | bytes 3096584 | tf_op jit(solution)/shard_map/ppermute | solution.py:26
  486.1 66.7 %collective-permute-start.87 = (bf16[4,1008,128]{2,1,0:T(8,128)(2,1)}, bf16[4,1008,128]{2,1,0:T(8,128)(2,1)}, u32[]{:S(2)}, u32[]{:S(2)}) collective-permute-start(bf16[4,1008,128]{2,1,0:T(8,128)(2,1)} %copy.462), channel_id=1, source_target_pairs={{0,48},{16,0},{32,16},{48,32},{1,49},{17,1},{33,17},{49,33},{2,50}... | collective-permute-start | bytes 3096584 | tf_op jit(solution)/shard_map/ppermute | solution.py:26
  500.1 61.0 %collective-permute-start.79 = (bf16[4,1008,128]{2,1,0:T(8,128)(2,1)}, bf16[4,1008,128]{2,1,0:T(8,128)(2,1)}, u32[]{:S(2)}, u32[]{:S(2)}) collective-permute-start(bf16[4,1008,128]{2,1,0:T(8,128)(2,1)} %copy.456), channel_id=1, source_target_pairs={{0,12},{1,13},{2,14},{3,15},{4,0},{5,1},{6,2},{7,3},{8,4},{9,5},{1... | collective-permute-start | bytes 3096584 | tf_op jit(solution)/shard_map/ppermute | solution.py:30
  501.3 62.0 %collective-permute-start.77 = (bf16[4,1008,128]{2,1,0:T(8,128)(2,1)}, bf16[4,1008,128]{2,1,0:T(8,128)(2,1)}, u32[]{:S(2)}, u32[]{:S(2)}) collective-permute-start(bf16[4,1008,128]{2,1,0:T(8,128)(2,1)} %copy.452), channel_id=1, source_target_pairs={{0,4},{1,5},{2,6},{3,7},{4,8},{5,9},{6,10},{7,11},{8,12},{9,13},{1... | collective-permute-start | bytes 3096584 | tf_op jit(solution)/shard_map/ppermute | solution.py:30
  548.3 21.3 %collective-permute-start.52 = (bf16[384,1024]{1,0:T(8,128)(2,1)}, bf16[384,1024]{1,0:T(8,128)(2,1)}, u32[]{:S(2)}, u32[]{:S(2)}) collective-permute-start(bf16[384,1024]{1,0:T(8,128)(2,1)} %convolution_convert_fusion.6), channel_id=1, source_target_pairs={{0,1},{1,0},{2,3},{3,2},{4,5},{5,4},{6,7},{7,6},{8,9},{9,8},{10,11... | collective-permute-start | bytes 2359304 | tf_op jit(solution)/shard_map/ppermute | solution.py:18
  557.9 44.0 %collective-permute-start.90 = (bf16[512,128]{0,1:T(8,128)(2,1)}, bf16[512,128]{0,1:T(8,128)(2,1)}, u32[]{:S(2)}, u32[]{:S(2)}) collective-permute-start(bf16[512,128]{0,1:T(8,128)(2,1)} %get-tuple-element.110), channel_id=1, source_target_pairs={{0,12},{1,13},{2,14},{3,15},{4,0},{5,1},{6,2},{7,3},{8,4},{9,5},{1... | collective-permute-start | bytes 393224 | tf_op jit(solution)/shard_map/ppermute | solution.py:30
  561.0 35.2 %collective-permute-start.88 = (bf16[496,128]{0,1:T(8,128)(2,1)}, bf16[496,128]{0,1:T(8,128)(2,1)}, u32[]{:S(2)}, u32[]{:S(2)}) collective-permute-start(bf16[496,128]{0,1:T(8,128)(2,1)} %get-tuple-element.107), channel_id=1, source_target_pairs={{0,4},{1,5},{2,6},{3,7},{4,8},{5,9},{6,10},{7,11},{8,12},{9,13},{1... | collective-permute-start | bytes 380936 | tf_op jit(solution)/shard_map/ppermute | solution.py:30
  568.6 37.0 %collective-permute-start.82 = (bf16[512,128]{0,1:T(8,128)(2,1)}, bf16[512,128]{0,1:T(8,128)(2,1)}, u32[]{:S(2)}, u32[]{:S(2)}) collective-permute-start(bf16[512,128]{0,1:T(8,128)(2,1)} %get-tuple-element.106), channel_id=1, source_target_pairs={{0,48},{16,0},{32,16},{48,32},{1,49},{17,1},{33,17},{49,33},{2,50}... | collective-permute-start | bytes 393224 | tf_op jit(solution)/shard_map/ppermute | solution.py:26
  569.6 30.3 %collective-permute-start.80 = (bf16[496,128]{0,1:T(8,128)(2,1)}, bf16[496,128]{0,1:T(8,128)(2,1)}, u32[]{:S(2)}, u32[]{:S(2)}) collective-permute-start(bf16[496,128]{0,1:T(8,128)(2,1)} %get-tuple-element.103), channel_id=1, source_target_pairs={{0,16},{16,32},{32,48},{48,0},{1,17},{17,33},{33,49},{49,1},{2,18}... | collective-permute-start | bytes 380936 | tf_op jit(solution)/shard_map/ppermute | solution.py:26
  595.9 17.4 %collective-permute-start.66 = (bf16[2,544,128]{2,1,0:T(8,128)(2,1)S(1)}, bf16[2,544,128]{2,1,0:T(8,128)(2,1)S(1)}, u32[]{:S(2)}, u32[]{:S(2)}) collective-permute-start(bf16[2,544,128]{2,1,0:T(8,128)(2,1)S(1)} %pad_maximum_fusion.25), channel_id=1, source_target_pairs={{0,16},{16,32},{32,48},{48,0},{1,17},{17,33},{33,49},{49,1},{2,18}... | collective-permute-start | bytes 835592 | tf_op jit(solution)/shard_map/ppermute | solution.py:26
  596.3 19.7 %collective-permute-start.68 = (bf16[2,544,128]{2,1,0:T(8,128)(2,1)S(1)}, bf16[2,544,128]{2,1,0:T(8,128)(2,1)S(1)}, u32[]{:S(2)}, u32[]{:S(2)}) collective-permute-start(bf16[2,544,128]{2,1,0:T(8,128)(2,1)S(1)} %pad_maximum_fusion.26), channel_id=1, source_target_pairs={{0,48},{16,0},{32,16},{48,32},{1,49},{17,1},{33,17},{49,33},{2,50}... | collective-permute-start | bytes 835592 | tf_op jit(solution)/shard_map/ppermute | solution.py:26
  605.6 20.1 %collective-permute-start.57 = (bf16[2,96,512]{2,1,0:T(8,128)(2,1)S(1)}, bf16[2,96,512]{2,1,0:T(8,128)(2,1)S(1)}, u32[]{:S(2)}, u32[]{:S(2)}) collective-permute-start(bf16[2,96,512]{2,1,0:T(8,128)(2,1)S(1)} %fusion.148), channel_id=1, source_target_pairs={{0,1},{1,0},{2,3},{3,2},{4,5},{5,4},{6,7},{7,6},{8,9},{9,8},{10,11... | collective-permute-start | bytes 589832 | tf_op jit(solution)/shard_map/ppermute | solution.py:18
  613.0 17.2 %collective-permute-start.81 = (bf16[1008,128]{0,1:T(8,128)(2,1)}, bf16[1008,128]{0,1:T(8,128)(2,1)}, u32[]{:S(2)}, u32[]{:S(2)}) collective-permute-start(bf16[1008,128]{0,1:T(8,128)(2,1)} %pad_maximum_fusion.29), channel_id=1, source_target_pairs={{0,16},{16,32},{32,48},{48,0},{1,17},{17,33},{33,49},{49,1},{2,18}... | collective-permute-start | bytes 774152 | tf_op jit(solution)/shard_map/ppermute | solution.py:26
  622.3 17.7 %collective-permute-start.67 = (bf16[4,544,128]{2,1,0:T(8,128)(2,1)}, bf16[4,544,128]{2,1,0:T(8,128)(2,1)}, u32[]{:S(2)}, u32[]{:S(2)}) collective-permute-start(bf16[4,544,128]{2,1,0:T(8,128)(2,1)} %pad_maximum_fusion.18), channel_id=1, source_target_pairs={{0,16},{16,32},{32,48},{48,0},{1,17},{17,33},{33,49},{49,1},{2,18}... | collective-permute-start | bytes 1671176 | tf_op jit(solution)/shard_map/ppermute | solution.py:26
  622.3 17.7 %collective-permute-start.69 = (bf16[4,544,128]{2,1,0:T(8,128)(2,1)}, bf16[4,544,128]{2,1,0:T(8,128)(2,1)}, u32[]{:S(2)}, u32[]{:S(2)}) collective-permute-start(bf16[4,544,128]{2,1,0:T(8,128)(2,1)} %pad_maximum_fusion.19), channel_id=1, source_target_pairs={{0,48},{16,0},{32,16},{48,32},{1,49},{17,1},{33,17},{49,33},{2,50}... | collective-permute-start | bytes 1671176 | tf_op jit(solution)/shard_map/ppermute | solution.py:26
  (184 other events, 1848.6 us)
